TPU v7x, 32 devices: a whole 2x2x4 slice. The times are simulated.
32 devices in a mesh: seq: 16 (over z, y, core), head: 2 (over x).
Axes of the slice: x: 2, y: 2, z: 4, core: 2. Of those that a mesh axis runs over, the one named last changes fastest.
Arguments:
- queries: bfloat16 [4096, 8192], P(('seq', 'head')), may hold values from -6 to 6
- key_rows: bfloat16 [4096, 1024], P(('seq', 'head')), may hold values from -6 to 6
- value_rows: bfloat16 [4096, 1024], P(('seq', 'head')), may hold values from -6 to 6
- parent: int32 [32], replicated, may hold values from -1 to 30, as said below
Outputs:
- attended: bfloat16 [4096, 8192], P(('seq', 'head'))
Inputs may be any that keep to these rules, and one draw needn't show every extreme that they name: parent[b] is -1 exactly for block 0, otherwise an earlier block; the lineage of every block has at most 12 entries, and some block's lineage has exactly 12.
All inputs are finite; a program needn't handle non-finite values.
Results may differ from a plain program's by a relative error of at most 0.005.
Values may be sent and summed in bfloat16 or wider, within the bound.
A program may use at most 64 MiB of HBM per device.

v0:
```python
import functools
import math

import jax
import jax.numpy as jnp
from jax import lax
from jax.experimental import pallas as pl
from jax.experimental.pallas import tpu as pltpu
from jax.sharding import PartitionSpec as P

HEADS = 64
KV_HEADS = 8
HEAD_DIM = 128
BLOCK = 128
DEPTH = 12
GROUP = HEADS // KV_HEADS
CHUNKS = 1


def ancestry(parent, first_block, num_local):
    columns = lax.broadcasted_iota(jnp.int32, (num_local, parent.shape[0]), 1)
    current = first_block + jnp.arange(num_local, dtype=jnp.int32)
    lineage = [current]
    for generation in range(DEPTH - 1):
        located = jnp.sum(jnp.where(columns == current[:, None], parent[None, :], 0), axis=1)
        current = jnp.where(current >= 0, located, -1)
        lineage.append(current)
    return jnp.stack(lineage, axis=1)


def attention_kernel(lineage_ref, q_ref, *refs):
    key_refs, value_refs, out_ref = refs[:DEPTH], refs[DEPTH : 2 * DEPTH], refs[2 * DEPTH]
    block = pl.program_id(0)
    keys = jnp.concatenate([ref[...] for ref in key_refs], axis=0)
    values = jnp.concatenate([ref[...] for ref in value_refs], axis=0)
    factor = math.log2(math.e) / math.sqrt(HEAD_DIM)
    per_dot = 2
    rows = per_dot * BLOCK
    row = lax.rem(lax.broadcasted_iota(jnp.int32, (rows, BLOCK), 0), BLOCK)
    causal = lax.broadcasted_iota(jnp.int32, (rows, BLOCK), 1) <= row
    penalties = [
        jnp.where(lineage_ref[block, level] >= 0, 0.0, -jnp.inf).astype(jnp.float32)
        for level in range(DEPTH)
    ]
    for part in range(GROUP // per_dot):
        heads = range(part * per_dot, (part + 1) * per_dot)
        query = jnp.concatenate(
            [q_ref[:, head * HEAD_DIM : (head + 1) * HEAD_DIM] for head in heads], axis=0
        )
        scores = lax.dot_general(
            query, keys, (((1,), (1,)), ((), ())), preferred_element_type=jnp.float32
        )
        tiles = []
        for level in range(DEPTH):
            tile = scores[:, level * BLOCK : (level + 1) * BLOCK]
            if level == 0:
                tile = jnp.where(causal, tile, -jnp.inf)
            else:
                tile = tile + penalties[level]
            tiles.append(tile)
        peak = functools.reduce(jnp.maximum, tiles)
        peak = jnp.max(peak, axis=1, keepdims=True)
        weights = [jnp.exp2((tile - peak) * factor) for tile in tiles]
        total = jnp.sum(functools.reduce(jnp.add, weights), axis=1, keepdims=True)
        rounded = jnp.concatenate([weight.astype(jnp.bfloat16) for weight in weights], axis=1)
        result = jnp.dot(rounded, values, preferred_element_type=jnp.float32) / total
        for at, head in enumerate(heads):
            out_ref[:, head * HEAD_DIM : (head + 1) * HEAD_DIM] = result[
                at * BLOCK : (at + 1) * BLOCK
            ].astype(out_ref.dtype)


def attention(lineage, queries, keys, values, key_at, value_at, kv_heads):
    num_local = queries.shape[0] // BLOCK

    def tile_spec(level, first):
        return pl.BlockSpec(
            (BLOCK, HEAD_DIM),
            lambda block, head, lineage: (jnp.maximum(lineage[block, level], 0), first + head),
        )

    wide = pl.BlockSpec((BLOCK, GROUP * HEAD_DIM), lambda block, head, lineage: (block, head))
    return pl.pallas_call(
        attention_kernel,
        grid_spec=pltpu.PrefetchScalarGridSpec(
            num_scalar_prefetch=1,
            grid=(num_local, kv_heads),
            in_specs=[wide]
            + [tile_spec(level, key_at) for level in range(DEPTH)]
            + [tile_spec(level, value_at) for level in range(DEPTH)],
            out_specs=wide,
        ),
        out_shape=jax.ShapeDtypeStruct(queries.shape, jnp.bfloat16),
        compiler_params=pltpu.CompilerParams(vmem_limit_bytes=48 * 1024 * 1024),
        cost_estimate=pl.CostEstimate(
            flops=4 * queries.size * DEPTH * BLOCK,
            bytes_accessed=4 * queries.size + 4 * num_local * DEPTH * BLOCK * kv_heads * HEAD_DIM,
            transcendentals=queries.size * DEPTH,
        ),
    )(lineage, queries, *([keys] * DEPTH), *([values] * DEPTH))


def local_body(queries, key_rows, value_rows, parent):
    device = lax.axis_index("seq") * lax.axis_size("head") + lax.axis_index("head")
    num_local = queries.shape[0] // BLOCK
    lineage = ancestry(parent, device * num_local, num_local)
    both = jnp.concatenate([key_rows, value_rows], axis=1)
    gathered = lax.all_gather(both, ("seq", "head"), axis=0, tiled=True)
    return attention(lineage, queries, gathered, gathered, 0, KV_HEADS, KV_HEADS)


def split_body(queries, key_rows, value_rows, parent):
    exchange = functools.partial(
        lax.all_to_all, axis_name="head", split_axis=1, concat_axis=0, tiled=True
    )
    kv_heads = KV_HEADS // lax.axis_size("head")
    q_local, k_local, v_local = exchange(queries), exchange(key_rows), exchange(value_rows)
    num_local = q_local.shape[0] // BLOCK
    lineage = ancestry(parent, lax.axis_index("seq") * num_local, num_local)
    keys = lax.all_gather(k_local, "seq", axis=0, tiled=True)
    values = lax.all_gather(v_local, "seq", axis=0, tiled=True)
    attended = attention(lineage, q_local, keys, values, 0, 0, kv_heads)
    return lax.all_to_all(attended, "head", split_axis=0, concat_axis=1, tiled=True)


def body(queries, key_rows, value_rows, parent):
    if queries.shape[0] % BLOCK == 0:
        return local_body(queries, key_rows, value_rows, parent)
    return split_body(queries, key_rows, value_rows, parent)


def solution(mesh):
    return jax.shard_map(
        body,
        mesh=mesh,
        in_specs=(
            P(("seq", "head"), None),
            P(("seq", "head"), None),
            P(("seq", "head"), None),
            P(),
        ),
        out_specs=P(("seq", "head"), None),
        check_vma=False,
    )
```

profile of v0, /device:TPU:0, one launch (start us, length us, event | category | flops | bytes accessed | tf_op | source)
XLA Modules:
  0.0 165.3 jit_solution(9174021676609114394)
XLA Ops:
  6.5 0.0 all-gather.2.cloned.1.call-start
  6.5 1.9 %pad_maximum_fusion = bf16[128,2048]{1,0:T(8,128)(2,1)} fusion(bf16[128,1024]{1,0:T(8,128)(2,1)} %param.6, bf16[128,1024]{1,0:T(8,128)(2,1)} %param.5), kind=kLoop, calls=%fused_computation | loop fusion | flops 1048576 | bytes 1048576 | tf_op jit(solution)/shard_map/concatenate | solution.py:107
  8.4 0.0 all-gather.2.cloned.1.call-update
  8.4 1.3 fusion
  10.4 1.4 fusion.1
  12.4 1.3 fusion.2
  14.3 1.4 fusion.3
  16.4 1.3 fusion.4
  18.2 1.3 fusion.5
  20.1 1.4 fusion.6
  22.1 1.3 fusion.7
  24.1 1.3 fusion.8
  26.0 1.3 fusion.9
  28.0 1.3 fusion.10
  29.9 0.1 stack.47.lineage_ref
  30.0 97.9 %all-gather.2.cloned.1.call-done.refs_0_.refs_1_.refs_2_.refs_3_.refs_4_.refs_5_.refs_6_.refs_7_.refs_8_.refs_9_.refs_10_.refs_11_.refs_12_.refs_13_.refs_14_.refs_15_.refs_16_.refs_17_.refs_18_.refs_19_.refs_20_.refs_21_.refs_22_.refs_23_ = bf16[4096,2048]{1,0:T(8,128)(2,1)} async-done(((bf16[128,2048]{1,0:T(8,128)(2,1)}), bf16[4096,2048]{1,0:T(8,128)(2,1)}) %all-gather.2.cloned.1.call-update) | async-done | bytes 16777232 | tf_op jit(solution)/shard_map/all_gather | solution.py:108
  127.9 0.0 copy-start
  127.9 1.6 copy-done
  129.5 28.9 %shard_map.46 = bf16[128,8192]{1,0:T(8,128)(2,1)} custom-call(s32[1,12]{1,0:T(1,128)S(1)} %stack.47.lineage_ref, bf16[128,8192]{1,0:T(8,128)(2,1)S(1)} %copy-done, ...), custom_call_target="tpu_custom_call" | custom-call | flops 6442450944 | bytes 10485760 | tf_op jit(solution)/shard_map/pallas_call | solution.py:83
Async XLA Ops:
  6.5 121.4 %all-gather.2.cloned.1.call-start = ((), (), s32[]{:S(2)}) async-start(), calls=%async_computation | async-start | bytes 17301504 | tf_op jit(solution)/shard_map/all_gather | solution.py:108
  127.9 1.6 copy-start
Sparse Core Ops, SparseCore 0:
  10.4 117.5 all-gather.1
where the time goes:
time: 166 us; the launch traced here: 165 us
  waiting for transfers between devices  97.9 us (59%)
  Pallas kernels  28.9 us (17%)
  between operations  20.3 us (12%)
  other arithmetic  16.4 us (10%)
  local copies, waits for them, and re-layouts  1.7 us (1%)
    all_gather x1, waiting for transfers between devices, local_body(): gathered = lax.all_gather(both, ('seq', 'head'), axis=0, tiled=True)  97.9 us
    pallas_call x1, Pallas kernels, attention(): pl.pallas_call(attention_kernel, grid_spec=pltpu.PrefetchScalarGridSpec(n...  28.9 us
    reduce_sum x11, other arithmetic, ancestry(): jnp.sum(jnp.where(columns == current[:, None], parent[None, :], 0), axis=1)  14.5 us
  transfers between devices with their start and end apart: 1, of which 1 were waited for; matrix products, arithmetic and copies ran while one was open for 9% of the time, Pallas kernels for 0%

commit v1 on v0

--- a/solution.py
+++ b/solution.py
@@ -14,7 +14,10 @@
 BLOCK = 128
 DEPTH = 12
 GROUP = HEADS // KV_HEADS
-CHUNKS = 1
+CHUNKS = 4
+PER_DOT = 2
+PORTIONS = 2
+MESH = pl.DeviceIdType.MESH
 
 
 def ancestry(parent, first_block, num_local):
@@ -100,13 +103,236 @@
     )(lineage, queries, *([keys] * DEPTH), *([values] * DEPTH))
 
 
-def local_body(queries, key_rows, value_rows, parent):
-    device = lax.axis_index("seq") * lax.axis_size("head") + lax.axis_index("head")
-    num_local = queries.shape[0] // BLOCK
-    lineage = ancestry(parent, device * num_local, num_local)
-    both = jnp.concatenate([key_rows, value_rows], axis=1)
-    gathered = lax.all_gather(both, ("seq", "head"), axis=0, tiled=True)
-    return attention(lineage, queries, gathered, gathered, 0, KV_HEADS, KV_HEADS)
+def fused_kernel(planes, parent_ref, q_ref, k_ref, v_ref, out_ref, *scratch):
+    buffers, (send_sems, recv_sems) = scratch[:CHUNKS], scratch[CHUNKS:]
+    seq, x = lax.axis_index("seq"), lax.axis_index("head")
+    z, y, core = seq // 4, lax.rem(seq // 2, 2), lax.rem(seq, 2)
+    block = seq * 2 + x
+    rows = q_ref.shape[0]
+    width = KV_HEADS * HEAD_DIM // (2 * CHUNKS)
+
+    def place(zz, yy, cc, xx):
+        return (zz * 4 + yy * 2 + cc, xx)
+
+    above, below = place(z + 1, y, core, x), place(z - 1, y, core, x)
+    across_x, across_y = place(z, y, core, 1 - x), place(z, 1 - y, core, x)
+    sibling = place(z, y, 1 - core, x)
+
+    barrier = pltpu.get_barrier_semaphore()
+
+    def greet(target):
+        pl.semaphore_signal(barrier, inc=1, device_id=target, device_id_type=MESH)
+
+    for target in (across_x, across_y, sibling):
+        greet(target)
+
+    @pl.when(z > 0)
+    def _():
+        greet(below)
+
+    @pl.when(z < planes - 1)
+    def _():
+        greet(above)
+
+    for chunk in range(CHUNKS):
+        for part in range(4):
+            source = (k_ref, v_ref)[part % 2]
+            first, second = ((x, y), (y, x))[part % 2]
+            at = (chunk * 2 + part // 2) * width
+            slot = z * 8 + core * 4 + second * 2 + first
+            buffers[chunk][part, slot] = source[:, at : at + width]
+
+    lineage = [block]
+    for level in range(DEPTH - 1):
+        found = parent_ref[jnp.maximum(lineage[-1], 0)]
+        lineage.append(jnp.where(lineage[-1] >= 0, found, -1))
+    penalties = [jnp.where(b >= 0, 0.0, -jnp.inf).astype(jnp.float32) for b in lineage]
+    clipped = [jnp.maximum(b, 0) for b in lineage]
+    key_slots, value_slots = [], []
+    for b in clipped:
+        bz, by, bc, bx = b // 8, lax.rem(b // 4, 2), lax.rem(b // 2, 2), lax.rem(b, 2)
+        key_slots.append(bz * 8 + bc * 4 + by * 2 + bx)
+        value_slots.append(bz * 8 + bc * 4 + bx * 2 + by)
+
+    pl.semaphore_wait(barrier, 3 + (z > 0).astype(jnp.int32) + (z < planes - 1).astype(jnp.int32))
+
+    def copy(chunk, part, zz, stage, slot, count, target):
+        span = buffers[chunk].at[part, pl.ds(slot, count)]
+        return pltpu.make_async_remote_copy(
+            src_ref=span,
+            dst_ref=span,
+            send_sem=send_sems.at[chunk, part, zz, stage],
+            recv_sem=recv_sems.at[chunk, part, zz, stage],
+            device_id=target,
+            device_id_type=MESH,
+        )
+
+    def routes(part):
+        if part % 2 == 0:
+            return x, y, across_x, across_y
+        return y, x, across_y, across_x
+
+    def hop_up(chunk, part, zz):
+        first, second, _, _ = routes(part)
+        base = zz * 8 + core * 4 + second * 2
+        if part < 2:
+            return copy(chunk, part, zz, 0, base + first, 1, above)
+        return copy(chunk, part, zz, 0, base, 2, above)
+
+    def hop_first(chunk, part, zz, mine):
+        first, second, target, _ = routes(part)
+        at = first if mine else 1 - first
+        return copy(chunk, part, zz, 1, zz * 8 + core * 4 + second * 2 + at, 1, target)
+
+    def hop_second(chunk, part, zz, mine):
+        _, second, _, target = routes(part)
+        at = second if mine else 1 - second
+        return copy(chunk, part, zz, 2, zz * 8 + core * 4 + at * 2, 2, target)
+
+    def hop_core(chunk, part, zz, mine):
+        at = core if mine else 1 - core
+        return copy(chunk, part, zz, 3, zz * 8 + at * 4, 4, sibling)
+
+    def rise(chunk, part, zz):
+        @pl.when(z < planes - 1)
+        def _():
+            hop_up(chunk, part, zz).start()
+
+    def step_a(chunk, age):
+        zz = z - age
+        for part in (2, 3, 0, 1):
+            if age > 0:
+                hop_up(chunk, part, zz).wait_recv()
+            if part < 2:
+                rise(chunk, part, zz)
+                hop_first(chunk, part, zz, True).start()
+            elif age == 0:
+                hop_first(chunk, part, zz, True).start()
+            else:
+                rise(chunk, part, zz)
+                hop_second(chunk, part, zz, True).start()
+
+    def step_b(chunk, age):
+        zz = z - age
+        for part in (2, 3, 0, 1):
+            if part < 2 or age == 0:
+                hop_first(chunk, part, zz, False).wait_recv()
+                if part >= 2:
+                    rise(chunk, part, zz)
+                hop_second(chunk, part, zz, True).start()
+
+    def step_c(chunk, age):
+        for part in (2, 3, 0, 1):
+            hop_second(chunk, part, z - age, False).wait_recv()
+            hop_core(chunk, part, z - age, True).start()
+
+    def step_d(chunk, age):
+        for part in (2, 3, 0, 1):
+            hop_core(chunk, part, z - age, False).wait_recv()
+
+    def guarded(step, chunk, age):
+        if age == 0:
+            step(chunk, age)
+        else:
+            pl.when(z >= age)(functools.partial(step, chunk, age))
+
+    factor = math.log2(math.e) / math.sqrt(HEAD_DIM)
+    wide_rows = PER_DOT * rows
+    row = lax.rem(lax.broadcasted_iota(jnp.int32, (wide_rows, BLOCK), 0), BLOCK)
+    causal = lax.broadcasted_iota(jnp.int32, (wide_rows, BLOCK), 1) <= row
+
+    def attend(chunk, kv_head, portion):
+        pair, lane = divmod(kv_head, width // HEAD_DIM)
+        lanes = pl.ds(lane * HEAD_DIM, HEAD_DIM)
+        buffer = buffers[chunk]
+        keys = jnp.concatenate([buffer[2 * pair, slot, :, lanes] for slot in key_slots], axis=0)
+        values = jnp.concatenate(
+            [buffer[2 * pair + 1, slot, :, lanes] for slot in value_slots], axis=0
+        )
+        first_head = (chunk * (KV_HEADS // CHUNKS) + kv_head) * GROUP
+        dots = GROUP // PER_DOT // PORTIONS
+        for dot_at in range(portion * dots, (portion + 1) * dots):
+            heads = [first_head + dot_at * PER_DOT + i for i in range(PER_DOT)]
+            query = jnp.concatenate(
+                [q_ref[:, head * HEAD_DIM : (head + 1) * HEAD_DIM] for head in heads], axis=0
+            )
+            scores = lax.dot_general(
+                query, keys, (((1,), (1,)), ((), ())), preferred_element_type=jnp.float32
+            )
+            tiles = []
+            for level in range(DEPTH):
+                tile = scores[:, level * BLOCK : (level + 1) * BLOCK]
+                if level == 0:
+                    tile = jnp.where(causal, tile, -jnp.inf)
+                else:
+                    tile = tile + penalties[level]
+                tiles.append(tile)
+            peak = jnp.max(functools.reduce(jnp.maximum, tiles), axis=1, keepdims=True)
+            weights = [jnp.exp2((tile - peak) * factor) for tile in tiles]
+            total = jnp.sum(functools.reduce(jnp.add, weights), axis=1, keepdims=True)
+            rounded = jnp.concatenate([w.astype(jnp.bfloat16) for w in weights], axis=1)
+            result = jnp.dot(rounded, values, preferred_element_type=jnp.float32) / total
+            for i, head in enumerate(heads):
+                out_ref[:, head * HEAD_DIM : (head + 1) * HEAD_DIM] = result[
+                    i * rows : (i + 1) * rows
+                ].astype(out_ref.dtype)
+
+    items = [(chunk, age) for chunk in range(CHUNKS) for age in range(planes)]
+    pending = []
+    for at in range(len(items) + 3):
+        for delay, step in ((3, step_d), (2, step_c), (1, step_b), (0, step_a)):
+            if 0 <= at - delay < len(items):
+                guarded(step, *items[at - delay])
+        if at >= 3 and items[at - 3][1] == planes - 1:
+            chunk = items[at - 3][0]
+            for kv_head in range(KV_HEADS // CHUNKS):
+                for portion in range(PORTIONS):
+                    pending.append((chunk, kv_head, portion))
+        for _ in range(-(-KV_HEADS * PORTIONS // len(items))):
+            if pending:
+                attend(*pending.pop(0))
+    for work in pending:
+        attend(*work)
+
+    for chunk in range(CHUNKS):
+        for age in range(planes):
+
+            def finish(chunk, age):
+                zz = z - age
+                for part in range(4):
+                    if part < 2 or age == 0:
+                        hop_first(chunk, part, zz, True).wait_send()
+                    hop_second(chunk, part, zz, True).wait_send()
+                    hop_core(chunk, part, zz, True).wait_send()
+
+                    @pl.when(z < planes - 1)
+                    def _():
+                        hop_up(chunk, part, zz).wait_send()
+
+            guarded(finish, chunk, age)
+
+
+def fused_body(queries, key_rows, value_rows, parent):
+    devices = lax.axis_size("seq") * lax.axis_size("head")
+    planes = devices // 8
+    width = KV_HEADS * HEAD_DIM // (2 * CHUNKS)
+    vmem = pl.BlockSpec(memory_space=pltpu.VMEM)
+    return pl.pallas_call(
+        functools.partial(fused_kernel, planes),
+        out_shape=jax.ShapeDtypeStruct(queries.shape, jnp.bfloat16),
+        in_specs=[pl.BlockSpec(memory_space=pltpu.SMEM), vmem, vmem, vmem],
+        out_specs=vmem,
+        scratch_shapes=[pltpu.VMEM((4, devices, BLOCK, width), jnp.bfloat16)] * CHUNKS
+        + [pltpu.SemaphoreType.DMA((CHUNKS, 4, planes, 4))] * 2,
+        compiler_params=pltpu.CompilerParams(
+            collective_id=0, has_side_effects=True, vmem_limit_bytes=56 * 1024 * 1024
+        ),
+        cost_estimate=pl.CostEstimate(
+            flops=4 * queries.size * DEPTH * BLOCK,
+            bytes_accessed=4 * queries.size,
+            transcendentals=queries.size * DEPTH,
+        ),
+    )(parent, queries, key_rows, value_rows)
 
 
 def split_body(queries, key_rows, value_rows, parent):
@@ -124,8 +350,9 @@
 
 
 def body(queries, key_rows, value_rows, parent):
-    if queries.shape[0] % BLOCK == 0:
-        return local_body(queries, key_rows, value_rows, parent)
+    seq, head = lax.axis_size("seq"), lax.axis_size("head")
+    if queries.shape[0] == BLOCK and head == 2 and seq % 4 == 0 and seq <= 16:
+        return fused_body(queries, key_rows, value_rows, parent)
     return split_body(queries, key_rows, value_rows, parent)
 
 

time: 166 us -> 111 us (0.67)
  the two profiles are of different devices: /device:TPU:0 before, /device:TPU:25 now
where the time goes in v1:
time: 111 us
  Pallas kernels  108 us (97%)
  local copies, waits for them, and re-layouts  3.1 us (3%)
    pallas_call x1, Pallas kernels, fused_body(): pl.pallas_call(functools.partial(fused_kernel, planes), out_shape=jax.Sha...  108 us
    unnamed x1, local copies, waits for them, and re-layouts  3.1 us

profile of v1, /device:TPU:25, one launch (start us, length us, event | category | flops | bytes accessed | tf_op | source)
XLA Modules:
  0.0 110.6 jit_solution(5984285559728755261)
XLA Ops:
  0.0 107.5 %shard_map.46 = bf16[128,8192]{1,0:T(8,128)(2,1)} custom-call(s32[32]{0:T(128)} %parent_ref.1, bf16[128,8192]{1,0:T(8,128)(2,1)} %q_ref.1, bf16[128,1024]{1,0:T(8,128)(2,1)} %k_ref.1, bf16[128,1024]{1,0:T(8,128)(2,1)} %v_ref.1), custom_call_target="tpu_custom_call" | custom-call | flops 6442450944 | bytes 4194304 | tf_op jit(solution)/shard_map/pallas_call | solution.py:320
  107.5 3.1 %copy.6 = bf16[128,8192]{1,0:T(8,128)(2,1)} copy(bf16[128,8192]{1,0:T(8,128)(2,1)} %shard_map.46) | data formatting | bytes 4194304

commit v2 on v1

--- a/solution.py
+++ b/solution.py
@@ -17,6 +17,7 @@
 CHUNKS = 4
 PER_DOT = 2
 PORTIONS = 2
+DIRECT = 4
 MESH = pl.DeviceIdType.MESH
 
 
@@ -175,7 +176,7 @@
     def hop_up(chunk, part, zz):
         first, second, _, _ = routes(part)
         base = zz * 8 + core * 4 + second * 2
-        if part < 2:
+        if part < DIRECT:
             return copy(chunk, part, zz, 0, base + first, 1, above)
         return copy(chunk, part, zz, 0, base, 2, above)
 
@@ -203,7 +204,7 @@
         for part in (2, 3, 0, 1):
             if age > 0:
                 hop_up(chunk, part, zz).wait_recv()
-            if part < 2:
+            if part < DIRECT:
                 rise(chunk, part, zz)
                 hop_first(chunk, part, zz, True).start()
             elif age == 0:
@@ -215,9 +216,9 @@
     def step_b(chunk, age):
         zz = z - age
         for part in (2, 3, 0, 1):
-            if part < 2 or age == 0:
+            if part < DIRECT or age == 0:
                 hop_first(chunk, part, zz, False).wait_recv()
-                if part >= 2:
+                if part >= DIRECT:
                     rise(chunk, part, zz)
                 hop_second(chunk, part, zz, True).start()
 
@@ -278,13 +279,14 @@
                 ].astype(out_ref.dtype)
 
     items = [(chunk, age) for chunk in range(CHUNKS) for age in range(planes)]
+    items.sort(key=lambda item: item[0] * 4 + item[1] * 2)
     pending = []
-    for at in range(len(items) + 3):
-        for delay, step in ((3, step_d), (2, step_c), (1, step_b), (0, step_a)):
+    for at in range(len(items) + 6):
+        for delay, step in ((6, step_d), (4, step_c), (2, step_b), (0, step_a)):
             if 0 <= at - delay < len(items):
                 guarded(step, *items[at - delay])
-        if at >= 3 and items[at - 3][1] == planes - 1:
-            chunk = items[at - 3][0]
+        if at >= 6 and items[at - 6][1] == planes - 1:
+            chunk = items[at - 6][0]
             for kv_head in range(KV_HEADS // CHUNKS):
                 for portion in range(PORTIONS):
                     pending.append((chunk, kv_head, portion))
@@ -300,7 +302,7 @@
             def finish(chunk, age):
                 zz = z - age
                 for part in range(4):
-                    if part < 2 or age == 0:
+                    if part < DIRECT or age == 0:
                         hop_first(chunk, part, zz, True).wait_send()
                     hop_second(chunk, part, zz, True).wait_send()
                     hop_core(chunk, part, zz, True).wait_send()

time: 111 us -> 94.1 us (0.85)
  Pallas kernels: 108 us -> 89.7 us
    pallas_call x1, Pallas kernels: 108 us -> 89.7 us  [fused_body(): pl.pallas_call(functools.partial(fused_kernel, planes), out_shape=jax.Sha...]
where the time goes in v2:
time: 94.1 us; the launch traced here: 92.8 us
  Pallas kernels  89.7 us (95%)
  local copies, waits for them, and re-layouts  3.1 us (3%)
    pallas_call x1, Pallas kernels, fused_body(): pl.pallas_call(functools.partial(fused_kernel, planes), out_shape=jax.Sha...  89.7 us
    unnamed x1, local copies, waits for them, and re-layouts  3.1 us

profile of v2, /device:TPU:25, one launch (start us, length us, event | category | flops | bytes accessed | tf_op | source)
XLA Modules:
  0.0 92.8 jit_solution(12329061842063887454)
XLA Ops:
  0.0 89.7 %shard_map.46 = bf16[128,8192]{1,0:T(8,128)(2,1)} custom-call(s32[32]{0:T(128)} %parent_ref.1, bf16[128,8192]{1,0:T(8,128)(2,1)} %q_ref.1, bf16[128,1024]{1,0:T(8,128)(2,1)} %k_ref.1, bf16[128,1024]{1,0:T(8,128)(2,1)} %v_ref.1), custom_call_target="tpu_custom_call" | custom-call | flops 6442450944 | bytes 4194304 | tf_op jit(solution)/shard_map/pallas_call | solution.py:322
  89.7 3.1 %copy.6 = bf16[128,8192]{1,0:T(8,128)(2,1)} copy(bf16[128,8192]{1,0:T(8,128)(2,1)} %shard_map.46) | data formatting | bytes 4194304
